TPU v7x, 32 devices: a whole 2x2x4 slice. The times are simulated.
32 devices in a mesh: grp: 2 (over x), patch: 8 (over z, y), head: 2 (over core).
Axes of the slice: x: 2, y: 2, z: 4, core: 2. Of those that a mesh axis runs over, the one named last changes fastest.
Arguments:
- queries: bfloat16 [4096, 1536], P(('grp', 'patch'), 'head'), parts along dimension 0, as said below
- fresh_pairs: bfloat16 [2, 4096, 1536], P(None, ('grp', 'patch'), 'head'), parts along dimension 1, may hold values from -5 to 5
- stale_pairs: bfloat16 [2, 2304, 1536], P(None, ('grp', 'patch'), 'head'), parts along dimension 1, as said below
- counts: int32 [16], P('grp'), parts along dimension 0, may hold values from 1 to 256, 1152 in all
- latents: bfloat16 [4096, 3072], P(('grp', 'patch'), 'head'), parts along dimension 0, may hold values from -6 to 6
- out_weight: bfloat16 [1536, 3072], P('head'), may hold values from -0.3125 to 0.3125
- gate: bfloat16 [6144], P(('grp', 'head')), parts along dimension 0, may hold values from 0.5 to 2
Outputs:
- mixed: bfloat16 [4096, 3072], P(('grp', 'patch'), 'head'), parts along dimension 0
There are 2 independent parts, one for each index of `grp`. A program takes and returns all parts, laid end to end along the dimension named above; an argument that names none is the same for every part. Nothing has to cross between parts.
Inputs may be any that keep to these rules, and one draw needn't show every extreme that they name: `queries`: every entry lies within -160 and 160. `stale_pairs`: every entry lies within -6 and 6. Device p of the patch axis holds live tokens in its first counts[p] slots; the counts sum to 1152.
All inputs are finite; a program needn't handle non-finite values.
Results may differ from a plain program's by a relative error of at most 0.009.
Values may be sent and summed in bfloat16 or wider, within the bound.
A program may use at most 192 MiB of HBM per device.

v0:
```python
import jax
import jax.numpy as jnp
from jax import lax
from jax.sharding import PartitionSpec as P

HEAD_DIM = 128


masked_score = -1e30


def stale_mask(length, low, high):
    rows = jnp.arange(length, dtype=jnp.int32)
    return (rows < low) | (rows >= high)


def local(queries, fresh_pairs, stale_pairs, counts, latents, out_weight, gate):
    slots = queries.shape[0]
    width = HEAD_DIM
    myself = lax.axis_index("patch")
    factor = 1.0 / float(width) ** 0.5
    offsets = jnp.cumsum(counts) - counts
    low = offsets[myself]
    high = low + counts[myself]
    query = queries.reshape(slots, -1, width)
    own_keys = fresh_pairs[0].reshape(slots, -1, width)
    own_values = fresh_pairs[1].reshape(slots, -1, width)
    own_live = jnp.arange(slots, dtype=jnp.int32) < counts[myself]
    own_scores = (
        jnp.einsum("qhd,khd->hqk", query, own_keys, preferred_element_type=jnp.float32) * factor
    )
    own_scores = jnp.where(own_live[None, None, :], own_scores, masked_score)
    top = jnp.max(own_scores, axis=-1)
    weights = jnp.exp(own_scores - top[:, :, None])
    total = jnp.sum(weights, axis=-1)
    summed = jnp.einsum(
        "hqk,khd->hqd", weights.astype(jnp.bfloat16), own_values, preferred_element_type=jnp.float32
    )
    piece = lax.all_gather(stale_pairs, "patch", axis=1, tiled=True)
    run_sum = summed
    length = piece.shape[1]
    keys = piece[0].reshape(length, -1, width)
    values = piece[1].reshape(length, -1, width)
    live = stale_mask(length, low, high)
    scores = jnp.einsum("qhd,khd->hqk", query, keys, preferred_element_type=jnp.float32) * factor
    scores = jnp.where(live[None, None, :], scores, masked_score)
    new_top = jnp.maximum(top, jnp.max(scores, axis=-1))
    shrink = jnp.exp(top - new_top)
    fresh_weights = jnp.exp(scores - new_top[:, :, None])
    new_total = total * shrink + jnp.sum(fresh_weights, axis=-1)
    added = jnp.einsum(
        "hqk,khd->hqd",
        fresh_weights.astype(jnp.bfloat16),
        values,
        preferred_element_type=jnp.float32,
    )
    summed = run_sum * shrink[:, :, None] + added
    attended = summed / new_total[:, :, None]
    attended = attended.transpose(1, 0, 2).reshape(slots, -1).astype(jnp.bfloat16)
    projected = jnp.dot(attended, out_weight, preferred_element_type=jnp.float32)
    shares = lax.psum_scatter(
        projected.astype(jnp.bfloat16), "head", scatter_dimension=1, tiled=True
    ).astype(jnp.float32)
    mixed = latents.astype(jnp.float32) + gate.astype(jnp.float32)[None, :] * shares
    return mixed.astype(jnp.bfloat16)


def solution(mesh):
    placed = (
        P(("grp", "patch"), "head"),
        P(None, ("grp", "patch"), "head"),
        P(None, ("grp", "patch"), "head"),
        P("grp"),
        P(("grp", "patch"), "head"),
        P("head", None),
        P(("grp", "head")),
    )
    return jax.shard_map(
        local, mesh=mesh, in_specs=placed, out_specs=P(("grp", "patch"), "head"), check_vma=False
    )
```

profile of v0, /device:TPU:0, one launch (start us, length us, event | category | flops | bytes accessed | tf_op | source)
XLA Modules:
  0.0 128.8 jit_solution(6163020948435345559)
XLA Ops:
  6.5 2.1 %copy.28 = bf16[2,144,768]{2,0,1:T(2,128)(2,1)} copy(bf16[2,144,768]{2,1,0:T(8,128)(2,1)} %param.9) | data formatting | bytes 884736 | tf_op args[2]
  8.7 0.8 reduce-window.9
  9.6 1.3 %dynamic_slice.7 = s32[1]{0:T(128)} dynamic-slice(s32[8]{0:T(128)} %param.10, s32[]{:T(128)S(6)} %select_n.13), dynamic_slice_sizes={1} | dynamic-slice | bytes 12 | tf_op jit(solution)/shard_map/dynamic_slice | solution.py:28
  10.9 0.7 bitcast_subtract_fusion
  11.5 0.6 dynamic_slice.8
  12.1 1.2 copy.22
  13.3 1.3 %fusion.26 = (bf16[1,256,768]{2,1,0:T(8,128)(2,1)S(1)}, bf16[1,256,768]{2,1,0:T(8,128)(2,1)S(1)}) fusion(bf16[2,256,768]{2,1,0:T(8,128)(2,1)} %param.8), kind=kLoop, calls=%fused_computation.35 | loop fusion | bytes 1572864 | tf_op jit(solution)/shard_map/slice | solution.py:27
  14.8 1.0 copy.26
  17.0 0.7 iota_compare_fusion.2
  17.7 1.2 fusion.21
  18.9 0.4 fusion.27
  19.3 1.2 copy-done
  20.8 56.7 %all-gather.2.cloned.1.call-done = bf16[2,1152,768]{2,0,1:T(2,128)(2,1)} async-done(((bf16[2,144,768]{2,0,1:T(2,128)(2,1)}), bf16[2,1152,768]{2,0,1:T(2,128)(2,1)}) %all-gather.2.cloned.1.call-update) | async-done | bytes 3538960 | tf_op jit(solution)/shard_map/all_gather | solution.py:39
  77.4 8.7 %fusion.25 = (bf16[1,1152,768]{2,0,1:T(2,128)(2,1)S(1)}, bf16[1,1152,768]{2,0,1:T(2,128)(2,1)}) fusion(bf16[2,1152,768]{2,0,1:T(2,128)(2,1)} %all-gather.2.cloned.1.call-done), kind=kLoop, calls=%fused_computation.34 | loop fusion | bytes 7077888 | tf_op jit(solution)/shard_map/slice | solution.py:42
  86.1 8.5 %copy.32 = bf16[1,1152,768]{1,2,0:T(8,128)(2,1)} copy(bf16[1,1152,768]{2,0,1:T(2,128)(2,1)} %get-tuple-element.8) | data formatting | bytes 3538944 | tf_op jit(solution)/shard_map/slice | solution.py:43
  94.7 7.1 %copy.39 = bf16[1,1152,768]{1,2,0:T(8,128)(2,1)} copy(bf16[1,1152,768]{2,0,1:T(2,128)(2,1)S(1)} %get-tuple-element.7) | data formatting | bytes 3538944
  101.8 2.9 %fusion = (f32[6,256]{1,0:T(8,128)S(1)}, f32[6,256,1152]{2,1,0:T(8,128)S(1)}) fusion(pred[1152]{0:T(1024)(128)(4,1)} %fusion.21, bf16[256,6,128]{0,2,1:T(8,128)(2,1)} %bitcast.47, bf16[1152,6,128]{0,2,1:T(8,128)(2,1)} %bitcast.45), kind=kOutput, calls=%fused_computation.2 | convolution fusion | flops 458291712 | bytes 9247872 | tf_op jit(solution)/shard_map/qhd,khd->hqk/dot_general | solution.py:45
  104.7 1.7 %fusion.1 = f32[6,256]{1,0:T(8,128)S(1)} fusion(f32[6,256,1152]{2,1,0:T(8,128)S(1)} %get-tuple-element.14, f32[6,256]{1,0:T(8,128)S(1)} %max.18, pred[1152]{0:T(1024)(128)(4,1)S(1)} %copy-done.6), kind=kLoop, calls=%fused_computation.3 | loop fusion | flops 7076352 | bytes 7091328 | tf_op jit(solution)/shard_map/reduce_sum | solution.py:50
  106.5 1.8 %fusion.11 = f32[256,6,128]{0,2,1:T(8,128)S(1)} fusion(bf16[1152,6,128]{0,2,1:T(8,128)(2,1)S(1)} %bitcast.48, f32[6,256,1152]{2,1,0:T(8,128)S(1)} %get-tuple-element.14, f32[6,256]{1,0:T(8,128)S(1)} %max.18, pred[1152]{0:T(1024)(128)(4,1)S(1)} %copy-done.6), kind=kOutput, calls=%fused_computation.16 | convolution fusion | flops 460062720 | bytes 9641088 | tf_op jit(solution)/shard_map/hqk,khd->hqd/dot_general | solution.py:51
  108.3 0.4 fusion.17
  108.7 0.5 slice-done
  109.4 2.6 %convolution_convert_fusion = bf16[256,3072]{1,0:T(8,128)(2,1)} fusion(bf16[256,768]{0,1:T(8,128)(2,1)S(1)} %bitcast.50, bf16[768,3072]{1,0:T(8,128)(2,1)S(1)} %bitcast.44), kind=kOutput, calls=%fused_computation.5 | convolution fusion | flops 1208745984 | bytes 6684672 | tf_op jit(solution)/shard_map/dot_general | solution.py:60
  112.0 7.7 %reduce-scatter.2.cloned.1.call-done = bf16[256,1536]{1,0:T(8,128)(2,1)} async-done(((bf16[256,3072]{1,0:T(8,128)(2,1)}), bf16[256,1536]{1,0:T(8,128)(2,1)}) %reduce-scatter.2.cloned.1.call-update) | async-done | bytes 786448 | tf_op jit(solution)/shard_map/reduce_scatter | solution.py:61
  119.7 2.2 %add_convert_fusion = bf16[256,1536]{1,0:T(8,128)(2,1)} fusion(bf16[256,1536]{1,0:T(8,128)(2,1)} %reduce-scatter.2.cloned.1.call-done, bf16[256,1536]{1,0:T(8,128)(2,1)S(1)} %copy-done.4, f32[1536]{0:T(1024)S(1)} %convert_element_type.28), kind=kLoop, calls=%fused_computation.11 | loop fusion | flops 1966080 | bytes 2365440 | tf_op jit(solution)/shard_map/convert_element_type | solution.py:65
  (28 shorter events, 0.6 us)
Async XLA Ops:
  6.5 70.9 %all-gather.2.cloned.1.call-start = ((), (), s32[]{:S(2)}) async-start(), calls=%async_computation.1 | async-start | bytes 3981312 | tf_op jit(solution)/shard_map/all_gather | solution.py:39
  8.7 111.0 %reduce-scatter.2.cloned.1.call-start = ((), (), s32[]{:S(2)}) async-start(), calls=%async_computation.2 | async-start | bytes 2359296 | tf_op jit(solution)/shard_map/reduce_scatter | solution.py:61
  13.3 7.5 %copy-start.2 = (bf16[256,768]{0,1:T(8,128)(2,1)}, bf16[256,768]{0,1:T(8,128)(2,1)S(1)}, u32[]{:S(2)}) copy-start(bf16[256,768]{0,1:T(8,128)(2,1)S(1)} %copy.22) | copy-start | bytes 1179652
  19.3 1.2 copy-start
  101.8 2.9 %copy-start.6 = (pred[1152]{0:T(1024)(128)(4,1)S(1)}, pred[1152]{0:T(1024)(128)(4,1)}, u32[]{:S(2)}) copy-start(pred[1152]{0:T(1024)(128)(4,1)} %fusion.21) | copy-start | bytes 3460
  104.7 1.7 %copy-start.3 = (bf16[1,1152,768]{1,2,0:T(8,128)(2,1)S(1)}, bf16[1,1152,768]{1,2,0:T(8,128)(2,1)}, u32[]{:S(2)}) copy-start(bf16[1,1152,768]{1,2,0:T(8,128)(2,1)} %copy.32) | copy-start | bytes 5308420
  106.5 2.8 %slice-start = ((s8[4718592]{0:T(1024)(128)(4,1)}), s8[4194304]{0:T(1024)(128)(4,1)S(1)}, s32[]{:S(2)}) async-start(s8[4718592]{0:T(1024)(128)(4,1)} %bitcast.43), calls=%async_computation.3 | async-start | bytes 8388608
  106.5 1.8 %copy-start.1 = (f32[6,256,256]{1,2,0:T(8,128)S(1)}, f32[6,256,256]{1,2,0:T(8,128)}, u32[]{:S(2)}) copy-start(f32[6,256,256]{1,2,0:T(8,128)} %copy-done) | copy-start | bytes 4718596
  106.5 1.8 %copy-start.5 = (bf16[1,256,768]{1,2,0:T(8,128)(2,1)S(1)}, bf16[1,256,768]{1,2,0:T(8,128)(2,1)}, u32[]{:S(2)}) copy-start(bf16[1,256,768]{1,2,0:T(8,128)(2,1)} %copy.26) | copy-start | bytes 1179652
  106.5 2.9 %slice-start.1 = ((s8[4718592]{0:T(1024)(128)(4,1)}), s8[524288]{0:T(1024)(128)(4,1)S(1)}, s32[]{:S(2)}) async-start(s8[4718592]{0:T(1024)(128)(4,1)} %bitcast.43), calls=%async_computation.4 | async-start | bytes 1048576
  109.4 2.6 %copy-start.7 = (bf16[1536]{0:T(1024)(128)(2,1)S(1)}, bf16[1536]{0:T(1024)(128)(2,1)}, u32[]{:S(2)}) copy-start(bf16[1536]{0:T(1024)(128)(2,1)} %param.13) | copy-start | bytes 9220
  109.4 10.3 %copy-start.4 = (bf16[256,1536]{1,0:T(8,128)(2,1)S(1)}, bf16[256,1536]{1,0:T(8,128)(2,1)}, u32[]{:S(2)}) copy-start(bf16[256,1536]{1,0:T(8,128)(2,1)} %param.11) | copy-start | bytes 2359300
Sparse Core Ops, SparseCore 0:
  9.5 67.8 all-gather.1
  112.1 7.5 reduce-scatter.1
where the time goes:
time: 129 us
  waiting for transfers between devices  64.4 us (50%)
  local copies, waits for them, and re-layouts  33.8 us (26%)
  between operations  14.8 us (11%)
  matrix products  8.14 us (6%)
  other arithmetic  7.54 us (6%)
    all_gather x1, waiting for transfers between devices, local(): piece = lax.all_gather(stale_pairs, 'patch', axis=1, tiled=True)  56.7 us
    unnamed x24, local copies, waits for them, and re-layouts  12.4 us
    slice x1, local copies, waits for them, and re-layouts, local(): keys = piece[0].reshape(length, -1, width)  8.68 us
    slice x1, local copies, waits for them, and re-layouts, local(): values = piece[1].reshape(length, -1, width)  8.52 us
    reduce_scatter x1, waiting for transfers between devices, local(): lax.psum_scatter(projected.astype(jnp.bfloat16), 'head', scatter_dimensio...  7.68 us
    dot_general x1, matrix products, local(): jnp.einsum('qhd,khd->hqk', query, keys, preferred_element_type=jnp.float32)  2.93 us
    dot_general x1, matrix products, local(): jnp.dot(attended, out_weight, preferred_element_type=jnp.float32)  2.61 us
  transfers between devices with their start and end apart: 2, of which 2 were waited for; matrix products, arithmetic and copies ran while one was open for 7% of the time, Pallas kernels for 0%

commit v1 on v0

v1 whole, which is shorter than its diff:
```python
import functools
import math

import jax
import jax.numpy as jnp
from jax import lax
from jax.experimental import pallas as pl
from jax.experimental.pallas import tpu as pltpu
from jax.sharding import PartitionSpec as P

HEAD_DIM = 128
MASKED = -1e30
MESH = pl.DeviceIdType.MESH


def kernel(
    n, inner, counts_ref, q_hbm, fresh_hbm, stale_hbm, lat_hbm, w_hbm, gate_ref, out_hbm,
    q, fresh, slots, lat, w_own, w_other, top, total, acc, att_own, att_other, proj, mixed,
    local_sem, send_sem, recv_sem, w_sem, att_send, att_recv, out_sem,
):
    Z, Y = n // inner, inner
    grp, me, core = lax.axis_index("grp"), lax.axis_index("patch"), lax.axis_index("head")
    z, y = me // Y, me % Y
    rows = slots.shape[2]
    width = q.shape[1]
    heads = width // HEAD_DIM
    half = lat.shape[1]
    scale = math.log2(math.e) / HEAD_DIM ** 0.5
    cut = (rows // 3) // 16 * 16
    pieces = ((0, 0, rows, False), (1, cut, rows - cut, False), (1, 0, cut, True))
    other = (grp, me, 1 - core)

    def there(step):
        return (grp, me + step, core)

    sides = ((z > 0, -Y), (z < Z - 1, Y), (y > 0, -1), (y < Y - 1, 1))

    own_copy = pltpu.make_async_copy(stale_hbm, slots.at[me], local_sem.at[0])
    own_copy.start()
    q_copy = pltpu.make_async_copy(q_hbm, q, local_sem.at[1])
    q_copy.start()
    fresh_copy = pltpu.make_async_copy(fresh_hbm, fresh, local_sem.at[2])
    fresh_copy.start()

    barrier = pltpu.get_barrier_semaphore()
    for there_is, step in sides:
        @pl.when(there_is)
        def _():
            pl.semaphore_signal(barrier, inc=1, device_id=there(step), device_id_type=MESH)
    pl.semaphore_signal(barrier, inc=1, device_id=other, device_id_type=MESH)
    peers = jnp.int32(1)
    for there_is, _step in sides:
        peers = peers + there_is.astype(jnp.int32)
    pl.semaphore_wait(barrier, peers)

    def piece_copy(slot, k, side):
        kind, first, count, _ = pieces[k]
        ref = slots.at[slot, kind, pl.ds(first, count), :]
        return pltpu.make_async_remote_copy(
            src_ref=ref, dst_ref=ref, send_sem=send_sem.at[k, side, slot],
            recv_sem=recv_sem.at[k, slot], device_id=there(sides[side][1]), device_id_type=MESH,
        )

    def sends(zs, ys, k):
        y_first = pieces[k][3]
        down, up = (zs >= z) & (z > 0), (zs <= z) & (z < Z - 1)
        left, right = (ys >= y) & (y > 0), (ys <= y) & (y < Y - 1)
        if y_first:
            return down, up, left & (zs == z), right & (zs == z)
        return down & (ys == y), up & (ys == y), left, right

    def forward(zs, ys, k):
        slot = zs * Y + ys
        for side, goes in enumerate(sends(zs, ys, k)):
            @pl.when(goes)
            def _():
                piece_copy(slot, k, side).start()

    def arrive(zs, ys, k):
        piece_copy(zs * Y + ys, k, 0).wait_recv()
        forward(zs, ys, k)

    own_copy.wait()
    for k in range(3):
        forward(z, y, k)

    lat_copy = pltpu.make_async_copy(lat_hbm, lat, local_sem.at[3])
    lat_copy.start()
    mine = pl.ds(pl.multiple_of(core * half, half), half)
    theirs = pl.ds(pl.multiple_of((1 - core) * half, half), half)
    w_copy = pltpu.make_async_copy(w_hbm.at[:, mine], w_own, local_sem.at[4])
    w_copy.start()
    w_send = pltpu.make_async_remote_copy(
        src_ref=w_hbm.at[:, theirs], dst_ref=w_other, send_sem=w_sem.at[0], recv_sem=w_sem.at[1],
        device_id=other, device_id_type=MESH,
    )
    w_send.start()

    low = jnp.int32(0)
    own = jnp.int32(0)
    for p in range(n):
        count = counts_ref[p]
        low = low + jnp.where(p < me, count, 0)
        own = own + jnp.where(p == me, count, 0)
    high = low + own

    def part(key_of, value_of, dead, first):
        for h in range(heads):
            at = slice(h * HEAD_DIM, (h + 1) * HEAD_DIM)
            s = lax.dot_general(
                key_of(at), q[:, at], (((1,), (1,)), ((), ())), preferred_element_type=jnp.float32
            )
            s = jnp.where(dead, MASKED, s)
            peak = jnp.max(s, axis=0, keepdims=True)
            if not first:
                before = top[h]
                peak = jnp.maximum(before, peak)
            weights = jnp.exp2((s - peak) * scale)
            summed = jnp.sum(weights, axis=0, keepdims=True)
            added = lax.dot_general(
                value_of(at), weights.astype(jnp.bfloat16), (((0,), (0,)), ((), ())),
                preferred_element_type=jnp.float32,
            )
            top[h] = peak
            if first:
                total[h] = summed
                acc[h] = added
            else:
                shrink = jnp.exp2((before - peak) * scale)
                total[h] = total[h] * shrink + summed
                acc[h] = acc[h] * shrink + added

    def attend(zs, ys):
        slot = zs * Y + ys
        row = slot * rows + lax.broadcasted_iota(jnp.int32, (rows, q.shape[0]), 0)
        dead = (row >= low) & (row < high)
        part(lambda at: slots[slot, 0, :, at], lambda at: slots[slot, 1, :, at], dead, False)

    q_copy.wait()
    fresh_copy.wait()
    place = lax.broadcasted_iota(jnp.int32, (fresh.shape[1], q.shape[0]), 0)
    part(lambda at: fresh[0, :, at], lambda at: fresh[1, :, at], place >= own, True)

    def step(d, carry):
        for k in range(3):
            for sign in (-1, 1):
                zs = z + sign * d

                @pl.when((d >= 1) & (zs >= 0) & (zs < Z))
                def _():
                    arrive(zs, y, k)

        e = d - 1

        def along_y(t, carry):
            dy, sz, sy = t // 4 + 1, 2 * ((t // 2) % 2) - 1, 2 * (t % 2) - 1
            zs, ys = z + sz * e, y + sy * dy
            once = (e >= 1) | ((e == 0) & (sz == 1))

            @pl.when(once & (zs >= 0) & (zs < Z) & (ys >= 0) & (ys < Y))
            def _():
                for k in range(3):
                    arrive(zs, ys, k)
                attend(zs, ys)
            return carry

        lax.fori_loop(0, 4 * (Y - 1), along_y, 0)

        def along_z(t, carry):
            zs = z + (2 * t - 1) * d

            @pl.when(((d >= 1) | (t == 1)) & (zs >= 0) & (zs < Z))
            def _():
                attend(zs, y)
            return carry

        lax.fori_loop(0, 2, along_z, 0)
        return carry

    lax.fori_loop(0, Z + 1, step, 0)

    def att_copy(h):
        at = pl.ds(h * HEAD_DIM, HEAD_DIM)
        return pltpu.make_async_remote_copy(
            src_ref=att_own.at[:, at], dst_ref=att_other.at[:, at], send_sem=att_send.at[h],
            recv_sem=att_recv.at[h], device_id=other, device_id_type=MESH,
        )

    for h in range(heads):
        done = acc[h] / total[h]
        att_own[:, h * HEAD_DIM:(h + 1) * HEAD_DIM] = done.T.astype(jnp.bfloat16)
        att_copy(h).start()

    w_copy.wait()
    chunk = half // 3
    for c in range(3):
        at = slice(c * chunk, (c + 1) * chunk)
        proj[:, at] = jnp.dot(att_own[...], w_own[:, at], preferred_element_type=jnp.float32)
    lat_copy.wait()
    w_send.wait()
    for h in range(heads):
        att_copy(h).wait()
    outs = []
    for c in range(3):
        at = slice(c * chunk, (c + 1) * chunk)
        full = proj[:, at] + jnp.dot(
            att_other[...], w_other[:, at], preferred_element_type=jnp.float32
        )
        result = lat[:, at].astype(jnp.float32) + gate_ref[:, at].astype(jnp.float32) * full
        mixed[:, at] = result.astype(jnp.bfloat16)
        there_at = pl.ds(c * chunk, chunk)
        copy = pltpu.make_async_copy(mixed.at[:, there_at], out_hbm.at[:, there_at], out_sem.at[c])
        copy.start()
        outs.append(copy)

    def sent(slot, carry):
        zs, ys = slot // Y, slot % Y
        for k in range(3):
            for side, goes in enumerate(sends(zs, ys, k)):
                @pl.when(goes)
                def _():
                    piece_copy(slot, k, side).wait_send()
        return carry

    lax.fori_loop(0, n, sent, 0)
    for copy in outs:
        copy.wait()


def local(n, inner, queries, fresh_pairs, stale_pairs, counts, latents, out_weight, gate):
    slots, width = queries.shape
    rows = stale_pairs.shape[1]
    half = latents.shape[1]
    heads = width // HEAD_DIM
    bf16, f32 = jnp.bfloat16, jnp.float32
    anywhere = pl.BlockSpec(memory_space=pl.ANY)
    dma = pltpu.SemaphoreType.DMA
    return pl.pallas_call(
        functools.partial(kernel, n, inner),
        out_shape=jax.ShapeDtypeStruct((slots, half), bf16),
        in_specs=[pl.BlockSpec(memory_space=pltpu.SMEM)] + [anywhere] * 5
        + [pl.BlockSpec(memory_space=pltpu.VMEM)],
        out_specs=anywhere,
        scratch_shapes=[
            pltpu.VMEM((slots, width), bf16),
            pltpu.VMEM((2, slots, width), bf16),
            pltpu.VMEM((n, 2, rows, width), bf16),
            pltpu.VMEM((slots, half), bf16),
            pltpu.VMEM((width, half), bf16),
            pltpu.VMEM((width, half), bf16),
            pltpu.VMEM((heads, 1, slots), f32),
            pltpu.VMEM((heads, 1, slots), f32),
            pltpu.VMEM((heads, HEAD_DIM, slots), f32),
            pltpu.VMEM((slots, width), bf16),
            pltpu.VMEM((slots, width), bf16),
            pltpu.VMEM((slots, half), f32),
            pltpu.VMEM((slots, half), bf16),
            dma((5,)),
            dma((3, 4, n)),
            dma((3, n)),
            dma((2,)),
            dma((heads,)),
            dma((heads,)),
            dma((3,)),
        ],
        compiler_params=pltpu.CompilerParams(
            collective_id=0, has_side_effects=True, vmem_limit_bytes=56 * 2 ** 20
        ),
    )(counts, queries, fresh_pairs, stale_pairs, latents, out_weight, gate.reshape(1, -1))


def solution(mesh):
    n = mesh.shape["patch"]
    root = math.isqrt(n)
    inner = next(size for size in range(root, 0, -1) if n % size == 0)
    placed = (
        P(("grp", "patch"), "head"),
        P(None, ("grp", "patch"), "head"),
        P(None, ("grp", "patch"), "head"),
        P("grp"),
        P(("grp", "patch"), "head"),
        P("head", None),
        P(("grp", "head")),
    )
    return jax.shard_map(
        functools.partial(local, n, inner), mesh=mesh, in_specs=placed,
        out_specs=P(("grp", "patch"), "head"), check_vma=False,
    )
```

time: 129 us -> 51.5 us (0.40)
  waiting for transfers between devices: 64.4 us -> 0 us
  Pallas kernels: 0 us -> 47.9 us
  local copies, waits for them, and re-layouts: 33.8 us -> 3.35 us
  between operations: 14.8 us -> 0.01 us
  matrix products: 8.14 us -> 0 us
  other arithmetic: 7.54 us -> 0 us
    all_gather x1 -> x0, waiting for transfers between devices: 56.7 us -> none  [local(): piece = lax.all_gather(stale_pairs, 'patch', axis=1, tiled=True)]
    pallas_call x0 -> x1, Pallas kernels: none -> 47.9 us  [local(): pl.pallas_call(functools.partial(kernel, n, inner), out_shape=jax.ShapeDt...]
    slice x4 -> x0, local copies, waits for them, and re-layouts: 19.5 us -> none  [the longest x1 8.68 us: local(): keys = piece[0].reshape(length, -1, width)]
    unnamed x24 -> x1, local copies, waits for them, and re-layouts: 12.4 us -> 2.06 us
    dot_general x5 -> x0, matrix products: 8.14 us -> none  [the longest x1 2.93 us: local(): jnp.einsum('qhd,khd->hqk', query, keys, preferred_element_type=jnp.float32)]
    reduce_scatter x1 -> x0, waiting for transfers between devices: 7.68 us -> none  [local(): lax.psum_scatter(projected.astype(jnp.bfloat16), 'head', scatter_dimensio...]
    convert_element_type x2 -> x0, other arithmetic: 2.25 us -> none  [the longest x1 2.24 us: local(): return mixed.astype(jnp.bfloat16)]
    reduce_sum x2 -> x0, other arithmetic: 1.93 us -> none  [the longest x1 1.71 us: local(): new_total = total * shrink + jnp.sum(fresh_weights, axis=-1)]
  transfers between devices with their start and end apart: 2 -> 0, of which waited for: 2 -> 0; matrix products, arithmetic and copies ran while one was open for 7% -> 0% of each run, Pallas kernels for 0% -> 0%
where the time goes in v1:
time: 51.5 us; the launch traced here: 51.3 us
  Pallas kernels  47.9 us (93%)
  local copies, waits for them, and re-layouts  3.35 us (7%)
    pallas_call x1, Pallas kernels, local(): pl.pallas_call(functools.partial(kernel, n, inner), out_shape=jax.ShapeDt...  47.9 us
    unnamed x1, local copies, waits for them, and re-layouts  2.06 us
    reshape x1, local copies, waits for them, and re-layouts, local(): gate.reshape(1, -1)  1.28 us

profile of v1, /device:TPU:0, one launch (start us, length us, event | category | flops | bytes accessed | tf_op | source)
XLA Modules:
  0.0 51.3 jit_solution(5160324317748231744)
XLA Ops:
  0.0 1.3 %reshape.3.gate_ref = bf16[1,1536]{1,0:T(2,128)(2,1)} reshape(bf16[1536]{0:T(1024)(128)(2,1)} %param.13) | data formatting | bytes 6144 | tf_op jit(solution)/shard_map/reshape | solution.py:269
  1.3 47.9 %shard_map.73 = bf16[256,1536]{1,0:T(8,128)(2,1)} custom-call(s32[8]{0:T(128)} %counts_ref.1, bf16[256,768]{1,0:T(8,128)(2,1)} %q_hbm.1, bf16[2,256,768]{2,1,0:T(8,128)(2,1)} %fresh_hbm.1, bf16[2,144,768]{2,1,0:T(8,128)(2,1)} %stale_hbm.1, bf16[256,1536]{1,0:T(8,128)(2,1)} %lat_hbm.1, bf16[768,3072]{1,0:T(8,128)(2,1)} %w_hbm.1, bf16[1,1536]{1,0:T(2,128)(2,1)} %reshape.3.gate_ref), custom_call_target="tpu_custom_call" | custom-call | tf_op jit(solution)/shard_map/pallas_call | solution.py:238
  49.2 2.1 %copy.9 = bf16[256,1536]{1,0:T(8,128)(2,1)} copy(bf16[256,1536]{1,0:T(8,128)(2,1)} %shard_map.73) | data formatting | bytes 1572864

commit v2 on v1

--- a/solution.py
+++ b/solution.py
@@ -206,7 +206,7 @@
         full = proj[:, at] + jnp.dot(
             att_other[...], w_other[:, at], preferred_element_type=jnp.float32
         )
-        result = lat[:, at].astype(jnp.float32) + gate_ref[:, at].astype(jnp.float32) * full
+        result = lat[:, at].astype(jnp.float32) + gate_ref[at].astype(jnp.float32)[None, :] * full
         mixed[:, at] = result.astype(jnp.bfloat16)
         there_at = pl.ds(c * chunk, chunk)
         copy = pltpu.make_async_copy(mixed.at[:, there_at], out_hbm.at[:, there_at], out_sem.at[c])
@@ -266,7 +266,7 @@
         compiler_params=pltpu.CompilerParams(
             collective_id=0, has_side_effects=True, vmem_limit_bytes=56 * 2 ** 20
         ),
-    )(counts, queries, fresh_pairs, stale_pairs, latents, out_weight, gate.reshape(1, -1))
+    )(counts, queries, fresh_pairs, stale_pairs, latents, out_weight, gate)
 
 
 def solution(mesh):

time: 51.5 us -> 50.2 us (0.975)
  local copies, waits for them, and re-layouts: 3.35 us -> 2.06 us
    reshape x1 -> x0, local copies, waits for them, and re-layouts: 1.28 us -> none  [local(): gate.reshape(1, -1)]
where the time goes in v2:
time: 50.2 us; the launch traced here: 50 us
  Pallas kernels  47.9 us (95%)
  local copies, waits for them, and re-layouts  2.06 us (4%)
    pallas_call x1, Pallas kernels, local(): pl.pallas_call(functools.partial(kernel, n, inner), out_shape=jax.ShapeDt...  47.9 us
    unnamed x1, local copies, waits for them, and re-layouts  2.06 us

profile of v2, /device:TPU:0, one launch (start us, length us, event | category | flops | bytes accessed | tf_op | source)
XLA Modules:
  0.0 50.0 jit_solution(8622482061819699322)
XLA Ops:
  0.0 47.9 %shard_map.73 = bf16[256,1536]{1,0:T(8,128)(2,1)} custom-call(s32[8]{0:T(128)} %counts_ref.1, bf16[256,768]{1,0:T(8,128)(2,1)} %q_hbm.1, bf16[2,256,768]{2,1,0:T(8,128)(2,1)} %fresh_hbm.1, bf16[2,144,768]{2,1,0:T(8,128)(2,1)} %stale_hbm.1, bf16[256,1536]{1,0:T(8,128)(2,1)} %lat_hbm.1, bf16[768,3072]{1,0:T(8,128)(2,1)} %w_hbm.1, bf16[1536]{0:T(1024)(128)(2,1)} %gate_ref.1), custom_call_target="tpu_custom_call" | custom-call | tf_op jit(solution)/shard_map/pallas_call | solution.py:238
  47.9 2.1 %copy.9 = bf16[256,1536]{1,0:T(8,128)(2,1)} copy(bf16[256,1536]{1,0:T(8,128)(2,1)} %shard_map.73) | data formatting | bytes 1572864

commit v3 on v2

--- a/solution.py
+++ b/solution.py
@@ -27,7 +27,7 @@
     half = lat.shape[1]
     scale = math.log2(math.e) / HEAD_DIM ** 0.5
     cut = (rows // 3) // 16 * 16
-    pieces = ((0, 0, rows, False), (1, cut, rows - cut, False), (1, 0, cut, True))
+    pieces = ((1, 0, cut, True), (0, 0, cut, False), (0, cut, cut, False), (0, 2 * cut, rows - 2 * cut, False), (1, cut, cut, False), (1, 2 * cut, rows - 2 * cut, False))
     other = (grp, me, 1 - core)
 
     def there(step):
@@ -81,7 +81,7 @@
         forward(zs, ys, k)
 
     own_copy.wait()
-    for k in range(3):
+    for k in range(len(pieces)):
         forward(z, y, k)
 
     lat_copy = pltpu.make_async_copy(lat_hbm, lat, local_sem.at[3])
@@ -142,7 +142,7 @@
     part(lambda at: fresh[0, :, at], lambda at: fresh[1, :, at], place >= own, True)
 
     def step(d, carry):
-        for k in range(3):
+        for k in range(len(pieces)):
             for sign in (-1, 1):
                 zs = z + sign * d
 
@@ -159,7 +159,7 @@
 
             @pl.when(once & (zs >= 0) & (zs < Z) & (ys >= 0) & (ys < Y))
             def _():
-                for k in range(3):
+                for k in range(len(pieces)):
                     arrive(zs, ys, k)
                 attend(zs, ys)
             return carry
@@ -215,7 +215,7 @@
 
     def sent(slot, carry):
         zs, ys = slot // Y, slot % Y
-        for k in range(3):
+        for k in range(len(pieces)):
             for side, goes in enumerate(sends(zs, ys, k)):
                 @pl.when(goes)
                 def _():
@@ -256,8 +256,8 @@
             pltpu.VMEM((slots, half), f32),
             pltpu.VMEM((slots, half), bf16),
             dma((5,)),
-            dma((3, 4, n)),
-            dma((3, n)),
+            dma((6, 4, n)),
+            dma((6, n)),
             dma((2,)),
             dma((heads,)),
             dma((heads,)),

time: 50.2 us -> 49.2 us (0.980)
  Pallas kernels: 47.9 us -> 47 us
    pallas_call x1, Pallas kernels: 47.9 us -> 47 us  [local(): pl.pallas_call(functools.partial(kernel, n, inner), out_shape=jax.ShapeDt...]
where the time goes in v3:
time: 49.2 us; the launch traced here: 49 us
  Pallas kernels  47 us (96%)
  local copies, waits for them, and re-layouts  2.06 us (4%)
    pallas_call x1, Pallas kernels, local(): pl.pallas_call(functools.partial(kernel, n, inner), out_shape=jax.ShapeDt...  47 us
    unnamed x1, local copies, waits for them, and re-layouts  2.06 us

profile of v3, /device:TPU:0, one launch (start us, length us, event | category | flops | bytes accessed | tf_op | source)
XLA Modules:
  0.0 49.0 jit_solution(10682092545737087785)
XLA Ops:
  0.0 47.0 %shard_map.73 = bf16[256,1536]{1,0:T(8,128)(2,1)} custom-call(s32[8]{0:T(128)} %counts_ref.1, bf16[256,768]{1,0:T(8,128)(2,1)} %q_hbm.1, bf16[2,256,768]{2,1,0:T(8,128)(2,1)} %fresh_hbm.1, bf16[2,144,768]{2,1,0:T(8,128)(2,1)} %stale_hbm.1, bf16[256,1536]{1,0:T(8,128)(2,1)} %lat_hbm.1, bf16[768,3072]{1,0:T(8,128)(2,1)} %w_hbm.1, bf16[1536]{0:T(1024)(128)(2,1)} %gate_ref.1), custom_call_target="tpu_custom_call" | custom-call | tf_op jit(solution)/shard_map/pallas_call | solution.py:238
  47.0 2.1 %copy.9 = bf16[256,1536]{1,0:T(8,128)(2,1)} copy(bf16[256,1536]{1,0:T(8,128)(2,1)} %shard_map.73) | data formatting | bytes 1572864

commit v4 on v3

--- a/solution.py
+++ b/solution.py
@@ -16,6 +16,7 @@
 def kernel(
     n, inner, counts_ref, q_hbm, fresh_hbm, stale_hbm, lat_hbm, w_hbm, gate_ref, out_hbm,
     q, fresh, slots, lat, w_own, w_other, top, total, acc, att_own, att_other, proj, mixed,
+    held, shrunk,
     local_sem, send_sem, recv_sem, w_sem, att_send, att_recv, out_sem,
 ):
     Z, Y = n // inner, inner
@@ -136,6 +137,36 @@
         dead = (row >= low) & (row < high)
         part(lambda at: slots[slot, 0, :, at], lambda at: slots[slot, 1, :, at], dead, False)
 
+    def weigh(zs, ys):
+        slot = zs * Y + ys
+        row = slot * rows + lax.broadcasted_iota(jnp.int32, (rows, q.shape[0]), 0)
+        dead = (row >= low) & (row < high)
+        for h in range(heads):
+            at = slice(h * HEAD_DIM, (h + 1) * HEAD_DIM)
+            s = lax.dot_general(
+                slots[slot, 0, :, at], q[:, at], (((1,), (1,)), ((), ())),
+                preferred_element_type=jnp.float32,
+            )
+            s = jnp.where(dead, MASKED, s)
+            before = top[h]
+            peak = jnp.maximum(before, jnp.max(s, axis=0, keepdims=True))
+            weights = jnp.exp2((s - peak) * scale)
+            shrink = jnp.exp2((before - peak) * scale)
+            top[h] = peak
+            total[h] = total[h] * shrink + jnp.sum(weights, axis=0, keepdims=True)
+            shrunk[h] = shrink
+            held[h] = weights.astype(jnp.bfloat16)
+
+    def gather_values(zs, ys):
+        slot = zs * Y + ys
+        for h in range(heads):
+            at = slice(h * HEAD_DIM, (h + 1) * HEAD_DIM)
+            added = lax.dot_general(
+                slots[slot, 1, :, at], held[h], (((0,), (0,)), ((), ())),
+                preferred_element_type=jnp.float32,
+            )
+            acc[h] = acc[h] * shrunk[h] + added
+
     q_copy.wait()
     fresh_copy.wait()
     place = lax.broadcasted_iota(jnp.int32, (fresh.shape[1], q.shape[0]), 0)
@@ -159,9 +190,12 @@
 
             @pl.when(once & (zs >= 0) & (zs < Z) & (ys >= 0) & (ys < Y))
             def _():
-                for k in range(len(pieces)):
+                for k in range(4):
                     arrive(zs, ys, k)
-                attend(zs, ys)
+                weigh(zs, ys)
+                for k in range(4, len(pieces)):
+                    arrive(zs, ys, k)
+                gather_values(zs, ys)
             return carry
 
         lax.fori_loop(0, 4 * (Y - 1), along_y, 0)
@@ -255,6 +289,8 @@
             pltpu.VMEM((slots, width), bf16),
             pltpu.VMEM((slots, half), f32),
             pltpu.VMEM((slots, half), bf16),
+            pltpu.VMEM((heads, rows, slots), bf16),
+            pltpu.VMEM((heads, 1, slots), f32),
             dma((5,)),
             dma((6, 4, n)),
             dma((6, n)),

time: 49.2 us -> 48.9 us (level)
  no operation moved by 1% of the time
where the time goes in v4:
time: 48.9 us; the launch traced here: 48.8 us
  Pallas kernels  46.7 us (96%)
  local copies, waits for them, and re-layouts  2.06 us (4%)
    pallas_call x1, Pallas kernels, local(): pl.pallas_call(functools.partial(kernel, n, inner), out_shape=jax.ShapeDt...  46.7 us
    unnamed x1, local copies, waits for them, and re-layouts  2.06 us

profile of v4, /device:TPU:0, one launch (start us, length us, event | category | flops | bytes accessed | tf_op | source)
XLA Modules:
  0.0 48.8 jit_solution(6125274646221960055)
XLA Ops:
  0.0 46.7 %shard_map.73 = bf16[256,1536]{1,0:T(8,128)(2,1)} custom-call(s32[8]{0:T(128)} %counts_ref.1, bf16[256,768]{1,0:T(8,128)(2,1)} %q_hbm.1, bf16[2,256,768]{2,1,0:T(8,128)(2,1)} %fresh_hbm.1, bf16[2,144,768]{2,1,0:T(8,128)(2,1)} %stale_hbm.1, bf16[256,1536]{1,0:T(8,128)(2,1)} %lat_hbm.1, bf16[768,3072]{1,0:T(8,128)(2,1)} %w_hbm.1, bf16[1536]{0:T(1024)(128)(2,1)} %gate_ref.1), custom_call_target="tpu_custom_call" | custom-call | tf_op jit(solution)/shard_map/pallas_call | solution.py:272
  46.7 2.1 %copy.9 = bf16[256,1536]{1,0:T(8,128)(2,1)} copy(bf16[256,1536]{1,0:T(8,128)(2,1)} %shard_map.73) | data formatting | bytes 1572864
